TPU v7x, 256 devices: a whole 4x4x8 slice. The times are simulated.
256 devices in a mesh: grp: 128 (over x_lo, z, y, core), half: 2 (over x_hi).
Axes of the slice: x: 4 (x_hi: 2, x_lo: 2; x = x_hi * 2 + x_lo), y: 4, z: 8, core: 2. Of those that a mesh axis runs over, the one named last changes fastest.
Arguments:
- field: bfloat16 [128, 2, 1024, 512], P('grp', 'half'), may hold values from -6 to 6
- source_one: bfloat16 [128, 2, 4, 256, 256], P('grp', 'half'), may hold values from -0.375 to 0.375
- sections_one: bfloat16 [128, 2, 3, 4, 256, 512], P('grp', 'half'), may hold values from -0.25 to 0.25
- target_one: bfloat16 [128, 2, 4, 256, 256], P('grp', 'half'), may hold values from -0.375 to 0.375
- source_two: bfloat16 [128, 2, 4, 256, 256], P('grp', 'half'), may hold values from -0.375 to 0.375
- sections_two: bfloat16 [128, 2, 3, 4, 256, 512], P('grp', 'half'), may hold values from -0.25 to 0.25
- target_two: bfloat16 [128, 2, 4, 256, 256], P('grp', 'half'), may hold values from -0.375 to 0.375
- pairing: int32 [2, 3, 128, 2, 4], P(None, None, 'grp', 'half'), may hold values from 0 to 3, each once within a row
Outputs:
- scattered: bfloat16 [128, 2, 1024, 512], P('grp', 'half')
Inputs may be any that keep to these rules, and one draw needn't show every extreme that they name: For every level l, section s, group index g and half h, pairing[l, s, g, h] is a permutation of the 4 nodes.
All inputs are finite; a program needn't handle non-finite values.
Results may differ from a plain program's by a relative error of at most 0.007.
Values may be sent and summed in bfloat16 or wider, within the bound.
A program may use at most 64 MiB of HBM per device.

v0:
```python
import jax
import jax.numpy as jnp
from jax import lax
from jax.sharding import PartitionSpec as P

SECTIONS = 3


def swapped(value, axis, bit):
    return lax.ppermute(value, axis, [(i, i ^ 1 << bit) for i in range(lax.axis_size(axis))])


def product(basis, blocks):
    return jnp.einsum("nij,njc->nic", basis, blocks, preferred_element_type=jnp.float32)


def advance(coeffs, partner, weights, tables):
    partner = jnp.take(partner, tables, axis=0)
    stacked = jnp.concatenate([coeffs, partner], axis=1)
    return product(weights, stacked).astype(jnp.bfloat16)


def on_device(
    field, source_one, sections_one, target_one, source_two, sections_two, target_two, pairing
):
    node_count = source_one.shape[2]
    leaf_rows = source_one.shape[3]
    columns = field.shape[3]
    blocks = field.reshape(node_count, leaf_rows, columns)
    top_bit = lax.axis_size("grp").bit_length() - 1
    tables_one = pairing[0, :, 0, 0]
    tables_two = pairing[1, :, 0, 0]
    first = product(source_one[0, 0], blocks).astype(jnp.bfloat16)
    second = product(source_two[0, 0], blocks).astype(jnp.bfloat16)
    for section in range(SECTIONS):
        partner_one = swapped(first, "grp", top_bit - 1 - section)
        first = advance(first, partner_one, sections_one[0, 0, section], tables_one[section])
        partner_two = swapped(second, "grp", top_bit - 2 - section)
        second = advance(second, partner_two, sections_two[0, 0, section], tables_two[section])
    sibling = swapped(first, "half", 0)
    distant = swapped(second, "grp", top_bit - 1)
    total = product(target_one[0, 0], sibling) + product(target_two[0, 0], distant)
    return total.astype(jnp.bfloat16).reshape(field.shape)


def solution(mesh):
    placed = (
        P("grp", "half", None, None),
        P("grp", "half", None, None, None),
        P("grp", "half", None, None, None, None),
        P("grp", "half", None, None, None),
        P("grp", "half", None, None, None),
        P("grp", "half", None, None, None, None),
        P("grp", "half", None, None, None),
        P(None, None, "grp", "half", None),
    )
    return jax.shard_map(
        on_device,
        mesh=mesh,
        in_specs=placed,
        out_specs=P("grp", "half", None, None),
        check_vma=False,
    )
```

profile of v0, /device:TPU:1, one launch (start us, length us, event | category | flops | bytes accessed | tf_op | source)
XLA Modules:
  0.0 252.5 jit_solution(13113024503044727751)
XLA Ops:
  0.0 0.0 copy-start
  0.0 0.0 copy-start.3
  0.0 1.2 copy-done
  1.2 0.0 copy-start.6
  1.2 1.5 convolution_convert_fusion
  2.7 0.0 copy-start.1
  2.7 7.8 %collective-permute-start.4 = (bf16[4,256,512]{2,1,0:T(8,128)(2,1)S(1)}, bf16[4,256,512]{2,1,0:T(8,128)(2,1)}, u32[]{:S(2)}, u32[]{:S(2)}) collective-permute-start(bf16[4,256,512]{2,1,0:T(8,128)(2,1)S(1)} %convolution_convert_fusion), channel_id=1, source_target_pairs={{0,64},{2,66},{4,68},{6,70},{8,72},{10,74},{12,76},{14,78},{16,80}... | collective-permute-start | bytes 3145736 | tf_op jit(solution)/shard_map/ppermute | solution.py:10
  10.6 0.0 copy-done.3
  10.6 1.4 convolution_convert_fusion.1
  12.0 1.2 collective-permute-start
  13.2 0.0 copy-done.6
  13.2 0.0 copy-done.1
  13.2 25.8 %collective-permute-done.4 = bf16[4,256,512]{2,1,0:T(8,128)(2,1)} collective-permute-done((bf16[4,256,512]{2,1,0:T(8,128)(2,1)S(1)}, bf16[4,256,512]{2,1,0:T(8,128)(2,1)}, u32[]{:S(2)}, u32[]{:S(2)}) %collective-permute-start.4) | collective-permute-done | bytes 1048608 | tf_op jit(solution)/shard_map/ppermute | solution.py:10
  39.0 1.8 gather_fusion.3
  40.9 0.0 copy-start.2
  40.9 0.2 broadcast_select_fusion.2
  41.0 1.0 copy-done.2
  42.1 2.9 %fusion.51 = bf16[4,256,512]{2,1,0:T(8,128)(2,1)} fusion(bf16[4,256,512]{2,1,0:T(8,128)(2,1)S(1)} %broadcast_select_fusion.2, bf16[4,256,512]{2,1,0:T(8,128)(2,1)S(1)} %copy-done.2, bf16[1,1,3,4,256,512]{5,4,3,2,1,0:T(8,128)(2,1)} %param.15), kind=kOutput, calls=%fused_computation.42 | convolution fusion | flops 541589504 | bytes 4194304 | tf_op jit(solution)/shard_map/nij,njc->nic/dot_general | solution.py:14
  45.0 18.6 %collective-permute-start.5 = (bf16[4,256,512]{2,1,0:T(8,128)(2,1)}, bf16[4,256,512]{2,1,0:T(8,128)(2,1)}, u32[]{:S(2)}, u32[]{:S(2)}) collective-permute-start(bf16[4,256,512]{2,1,0:T(8,128)(2,1)} %fusion.51), channel_id=1, source_target_pairs={{0,32},{2,34},{4,36},{6,38},{8,40},{10,42},{12,44},{14,46},{16,48}... | collective-permute-start | bytes 3145736 | tf_op jit(solution)/shard_map/ppermute | solution.py:10
  63.6 0.0 collective-permute-done
  63.6 0.6 gather_fusion
  64.2 0.2 broadcast_select_fusion.5
  64.4 3.2 %fusion.42 = bf16[4,256,512]{2,1,0:T(8,128)(2,1)} fusion(bf16[4,256,512]{2,1,0:T(8,128)(2,1)S(1)} %broadcast_select_fusion.5, bf16[4,256,512]{2,1,0:T(8,128)(2,1)} %convolution_convert_fusion.1, bf16[1,1,3,4,256,512]{5,4,3,2,1,0:T(8,128)(2,1)} %param.12), kind=kOutput, calls=%fused_computation.39 | convolution fusion | flops 541589504 | bytes 4194304 | tf_op jit(solution)/shard_map/nij,njc->nic/dot_general | solution.py:14
  67.6 4.6 %collective-permute-start.1 = (bf16[4,256,512]{2,1,0:T(8,128)(2,1)}, bf16[4,256,512]{2,1,0:T(8,128)(2,1)S(1)}, u32[]{:S(2)}, u32[]{:S(2)}) collective-permute-start(bf16[4,256,512]{2,1,0:T(8,128)(2,1)} %fusion.42), channel_id=1, source_target_pairs={{0,64},{2,66},{4,68},{6,70},{8,72},{10,74},{12,76},{14,78},{16,80}... | collective-permute-start | bytes 3145736 | tf_op jit(solution)/shard_map/ppermute | solution.py:10
  72.2 81.3 %collective-permute-done.5 = bf16[4,256,512]{2,1,0:T(8,128)(2,1)} collective-permute-done((bf16[4,256,512]{2,1,0:T(8,128)(2,1)}, bf16[4,256,512]{2,1,0:T(8,128)(2,1)}, u32[]{:S(2)}, u32[]{:S(2)}) %collective-permute-start.5) | collective-permute-done | bytes 1048608 | tf_op jit(solution)/shard_map/ppermute | solution.py:10
  153.5 1.8 gather_fusion.4
  155.3 0.2 broadcast_select_fusion.1
  155.5 3.2 %fusion.54 = bf16[4,256,512]{2,1,0:T(8,128)(2,1)} fusion(bf16[4,256,512]{2,1,0:T(8,128)(2,1)S(1)} %broadcast_select_fusion.1, bf16[4,256,512]{2,1,0:T(8,128)(2,1)} %fusion.51, bf16[1,1,3,4,256,512]{5,4,3,2,1,0:T(8,128)(2,1)} %param.15), kind=kOutput, calls=%fused_computation.43 | convolution fusion | flops 541589504 | bytes 4194304 | tf_op jit(solution)/shard_map/nij,njc->nic/dot_general | solution.py:14
  158.7 0.0 collective-permute-start.6
  158.8 0.0 collective-permute-done.1
  158.8 0.6 gather_fusion.1
  159.4 0.2 broadcast_select_fusion.4
  159.5 3.2 %fusion.45 = bf16[4,256,512]{2,1,0:T(8,128)(2,1)} fusion(bf16[4,256,512]{2,1,0:T(8,128)(2,1)S(1)} %broadcast_select_fusion.4, bf16[4,256,512]{2,1,0:T(8,128)(2,1)} %fusion.42, bf16[1,1,3,4,256,512]{5,4,3,2,1,0:T(8,128)(2,1)} %param.12), kind=kOutput, calls=%fused_computation.40 | convolution fusion | flops 541589504 | bytes 4194304 | tf_op jit(solution)/shard_map/nij,njc->nic/dot_general | solution.py:14
  162.8 1.5 collective-permute-start.2
  164.3 34.9 %collective-permute-done.6 = bf16[4,256,512]{2,1,0:T(8,128)(2,1)} collective-permute-done((bf16[4,256,512]{2,1,0:T(8,128)(2,1)}, bf16[4,256,512]{2,1,0:T(8,128)(2,1)}, u32[]{:S(2)}, u32[]{:S(2)}) %collective-permute-start.6) | collective-permute-done | bytes 1048608 | tf_op jit(solution)/shard_map/ppermute | solution.py:10
  199.2 1.8 gather_fusion.5
  201.0 0.2 broadcast_select_fusion
  201.2 3.2 %fusion.57 = bf16[4,256,512]{2,1,0:T(8,128)(2,1)} fusion(bf16[4,256,512]{2,1,0:T(8,128)(2,1)S(1)} %broadcast_select_fusion, bf16[4,256,512]{2,1,0:T(8,128)(2,1)} %fusion.54, bf16[1,1,3,4,256,512]{5,4,3,2,1,0:T(8,128)(2,1)} %param.15), kind=kOutput, calls=%fused_computation.44 | convolution fusion | flops 541589504 | bytes 4194304 | tf_op jit(solution)/shard_map/nij,njc->nic/dot_general | solution.py:14
  204.4 1.2 collective-permute-start.7
  205.6 3.7 %collective-permute-done.2 = bf16[4,256,512]{2,1,0:T(8,128)(2,1)} collective-permute-done((bf16[4,256,512]{2,1,0:T(8,128)(2,1)}, bf16[4,256,512]{2,1,0:T(8,128)(2,1)}, u32[]{:S(2)}, u32[]{:S(2)}) %collective-permute-start.2) | collective-permute-done | bytes 1048608 | tf_op jit(solution)/shard_map/ppermute | solution.py:10
  209.3 1.8 gather_fusion.2
  211.1 0.2 broadcast_select_fusion.3
  211.3 0.0 copy-start.4
  211.3 2.3 fusion.48
  213.6 0.0 copy-start.5
  213.6 2.8 %collective-permute-start.3 = (bf16[4,256,512]{2,1,0:T(8,128)(2,1)S(1)}, bf16[4,256,512]{2,1,0:T(8,128)(2,1)S(1)}, u32[]{:S(2)}, u32[]{:S(2)}) collective-permute-start(bf16[4,256,512]{2,1,0:T(8,128)(2,1)S(1)} %fusion.48), channel_id=1, source_target_pairs={{0,1},{1,0},{2,3},{3,2},{4,5},{5,4},{6,7},{7,6},{8,9},{9,8},{10,11... | collective-permute-start | bytes 3145736 | tf_op jit(solution)/shard_map/ppermute | solution.py:10
  216.5 9.9 %collective-permute-done.7 = bf16[4,256,512]{2,1,0:T(8,128)(2,1)S(1)} collective-permute-done((bf16[4,256,512]{2,1,0:T(8,128)(2,1)}, bf16[4,256,512]{2,1,0:T(8,128)(2,1)S(1)}, u32[]{:S(2)}, u32[]{:S(2)}) %collective-permute-start.7) | collective-permute-done | bytes 1048608 | tf_op jit(solution)/shard_map/ppermute | solution.py:10
  226.4 0.0 copy-done.4
  226.4 0.4 fusion.72
  226.9 24.2 %collective-permute-done.3 = bf16[4,256,512]{2,1,0:T(8,128)(2,1)S(1)} collective-permute-done((bf16[4,256,512]{2,1,0:T(8,128)(2,1)S(1)}, bf16[4,256,512]{2,1,0:T(8,128)(2,1)S(1)}, u32[]{:S(2)}, u32[]{:S(2)}) %collective-permute-start.3) | collective-permute-done | bytes 1048608 | tf_op jit(solution)/shard_map/ppermute | solution.py:10
  251.1 0.0 copy-done.5
  251.1 1.4 add_convert_fusion
  (7 shorter events, 0.0 us)
Async XLA Ops:
  0.0 1.2 copy-start
  0.0 10.6 %copy-start.3 = (bf16[1,1,4,256,256]{4,3,2,1,0:T(8,128)(2,1)S(1)}, bf16[1,1,4,256,256]{4,3,2,1,0:T(8,128)(2,1)}, u32[]{:S(2)}) copy-start(bf16[1,1,4,256,256]{4,3,2,1,0:T(8,128)(2,1)} %param.11) | copy-start | bytes 1572868
  1.2 12.0 %copy-start.6 = (s32[2,3,1,1,4]{4,3,2,1,0:T(1,128)S(1)}, s32[2,3,1,1,4]{4,3,2,1,0:T(1,128)}, u32[]{:S(2)}) copy-start(s32[2,3,1,1,4]{4,3,2,1,0:T(1,128)} %param.17) | copy-start | bytes 292
  2.7 10.5 %copy-start.1 = (bf16[4,256,512]{2,1,0:T(8,128)(2,1)}, bf16[4,256,512]{2,1,0:T(8,128)(2,1)S(1)}, u32[]{:S(2)}) copy-start(bf16[4,256,512]{2,1,0:T(8,128)(2,1)S(1)} %convolution_convert_fusion) | copy-start | bytes 3145732
  2.7 36.3 %collective-permute-start.4 = (bf16[4,256,512]{2,1,0:T(8,128)(2,1)S(1)}, bf16[4,256,512]{2,1,0:T(8,128)(2,1)}, u32[]{:S(2)}, u32[]{:S(2)}) collective-permute-start(bf16[4,256,512]{2,1,0:T(8,128)(2,1)S(1)} %convolution_convert_fusion), channel_id=1, source_target_pairs={{0,64},{2,66},{4,68},{6,70},{8,72},{10,74},{12,76},{14,78},{16,80}... | collective-permute-start | bytes 3145736 | tf_op jit(solution)/shard_map/ppermute | solution.py:10
  12.0 51.6 %collective-permute-start = (bf16[4,256,512]{2,1,0:T(8,128)(2,1)}, bf16[4,256,512]{2,1,0:T(8,128)(2,1)S(1)}, u32[]{:S(2)}, u32[]{:S(2)}) collective-permute-start(bf16[4,256,512]{2,1,0:T(8,128)(2,1)} %convolution_convert_fusion.1), channel_id=1, source_target_pairs={{0,128},{2,130},{4,132},{6,134},{8,136},{10,138},{12,140},{14,142}... | collective-permute-start | bytes 3145736 | tf_op jit(solution)/shard_map/ppermute | solution.py:10
  40.9 1.2 copy-start.2
  45.0 108.5 %collective-permute-start.5 = (bf16[4,256,512]{2,1,0:T(8,128)(2,1)}, bf16[4,256,512]{2,1,0:T(8,128)(2,1)}, u32[]{:S(2)}, u32[]{:S(2)}) collective-permute-start(bf16[4,256,512]{2,1,0:T(8,128)(2,1)} %fusion.51), channel_id=1, source_target_pairs={{0,32},{2,34},{4,36},{6,38},{8,40},{10,42},{12,44},{14,46},{16,48}... | collective-permute-start | bytes 3145736 | tf_op jit(solution)/shard_map/ppermute | solution.py:10
  67.6 91.2 %collective-permute-start.1 = (bf16[4,256,512]{2,1,0:T(8,128)(2,1)}, bf16[4,256,512]{2,1,0:T(8,128)(2,1)S(1)}, u32[]{:S(2)}, u32[]{:S(2)}) collective-permute-start(bf16[4,256,512]{2,1,0:T(8,128)(2,1)} %fusion.42), channel_id=1, source_target_pairs={{0,64},{2,66},{4,68},{6,70},{8,72},{10,74},{12,76},{14,78},{16,80}... | collective-permute-start | bytes 3145736 | tf_op jit(solution)/shard_map/ppermute | solution.py:10
  158.7 40.4 %collective-permute-start.6 = (bf16[4,256,512]{2,1,0:T(8,128)(2,1)}, bf16[4,256,512]{2,1,0:T(8,128)(2,1)}, u32[]{:S(2)}, u32[]{:S(2)}) collective-permute-start(bf16[4,256,512]{2,1,0:T(8,128)(2,1)} %fusion.54), channel_id=1, source_target_pairs={{0,16},{2,18},{4,20},{6,22},{8,24},{10,26},{12,28},{14,30},{16,0},... | collective-permute-start | bytes 3145736 | tf_op jit(solution)/shard_map/ppermute | solution.py:10
  162.8 46.5 %collective-permute-start.2 = (bf16[4,256,512]{2,1,0:T(8,128)(2,1)}, bf16[4,256,512]{2,1,0:T(8,128)(2,1)}, u32[]{:S(2)}, u32[]{:S(2)}) collective-permute-start(bf16[4,256,512]{2,1,0:T(8,128)(2,1)} %fusion.45), channel_id=1, source_target_pairs={{0,32},{2,34},{4,36},{6,38},{8,40},{10,42},{12,44},{14,46},{16,48}... | collective-permute-start | bytes 3145736 | tf_op jit(solution)/shard_map/ppermute | solution.py:10
  204.4 22.0 %collective-permute-start.7 = (bf16[4,256,512]{2,1,0:T(8,128)(2,1)}, bf16[4,256,512]{2,1,0:T(8,128)(2,1)S(1)}, u32[]{:S(2)}, u32[]{:S(2)}) collective-permute-start(bf16[4,256,512]{2,1,0:T(8,128)(2,1)} %fusion.57), channel_id=1, source_target_pairs={{0,128},{2,130},{4,132},{6,134},{8,136},{10,138},{12,140},{14,142}... | collective-permute-start | bytes 3145736 | tf_op jit(solution)/shard_map/ppermute | solution.py:10
  211.3 15.1 %copy-start.4 = (bf16[1,1,4,256,256]{4,3,2,1,0:T(8,128)(2,1)S(1)}, bf16[1,1,4,256,256]{4,3,2,1,0:T(8,128)(2,1)}, u32[]{:S(2)}) copy-start(bf16[1,1,4,256,256]{4,3,2,1,0:T(8,128)(2,1)} %param.16) | copy-start | bytes 1572868
  213.6 37.5 %copy-start.5 = (bf16[1,1,4,256,256]{4,3,2,1,0:T(8,128)(2,1)S(1)}, bf16[1,1,4,256,256]{4,3,2,1,0:T(8,128)(2,1)}, u32[]{:S(2)}) copy-start(bf16[1,1,4,256,256]{4,3,2,1,0:T(8,128)(2,1)} %param.13) | copy-start | bytes 1572868
  213.6 37.5 %collective-permute-start.3 = (bf16[4,256,512]{2,1,0:T(8,128)(2,1)S(1)}, bf16[4,256,512]{2,1,0:T(8,128)(2,1)S(1)}, u32[]{:S(2)}, u32[]{:S(2)}) collective-permute-start(bf16[4,256,512]{2,1,0:T(8,128)(2,1)S(1)} %fusion.48), channel_id=1, source_target_pairs={{0,1},{1,0},{2,3},{3,2},{4,5},{5,4},{6,7},{7,6},{8,9},{9,8},{10,11... | collective-permute-start | bytes 3145736 | tf_op jit(solution)/shard_map/ppermute | solution.py:10
where the time goes:
time: 255 us; the launch traced here: 253 us
  waiting for transfers between devices  180 us (71%)
  starting transfers between devices  37.7 us (15%)
  matrix products  22.9 us (9%)
  local copies, waits for them, and re-layouts  10.9 us (4%)
    ppermute x8, waiting for transfers between devices, swapped(): lax.ppermute(value, axis, [(i, i ^ 1 << bit) for i in range(lax.axis_size...  180 us
    ppermute x8, starting transfers between devices, swapped(): lax.ppermute(value, axis, [(i, i ^ 1 << bit) for i in range(lax.axis_size...  37.7 us
    dot_general x10, matrix products, product(): jnp.einsum('nij,njc->nic', basis, blocks, preferred_element_type=jnp.floa...  22.9 us
    gather x6, local copies, waits for them, and re-layouts, advance(): partner = jnp.take(partner, tables, axis=0)  8.57 us
  transfers between devices with their start and end apart: 8, of which 6 were waited for; matrix products, arithmetic and copies ran while one was open for 12% of the time, Pallas kernels for 0%

commit v1 on v0

v1 whole, which is shorter than its diff:
```python
import functools

import jax
import jax.numpy as jnp
from jax import lax
from jax.experimental import pallas as pl
from jax.experimental.pallas import tpu as pltpu
from jax.sharding import PartitionSpec as P

SECTIONS = 3
STAGES = SECTIONS + 1
WIDTH = 128
MESH = pl.DeviceIdType.MESH
WINDOW = 2
ONE, TWO = 0, 1
CRITICAL = ((TWO, 0), (ONE, 1), (TWO, 1), (ONE, 2))


def flipped(index, bit):
    size = 1 << bit
    return index + size - 2 * size * ((index // size) % 2)


def arrivals(chunks):
    due = []
    span = 2.0
    for place, (level, stage) in enumerate(CRITICAL):
        for c in range(chunks):
            due.append((span * (chunks * place + c + 1), level, stage, c))
    for c in range(chunks):
        due.append((c + 1.0 + 0.1, ONE, 0, c))
        done = span * (2 * chunks + c + 1)
        due.append((done + 1.5 * span, TWO, 2, c))
        done = span * (3 * chunks + c + 1)
        due.append((done + 1.5 * span, ONE, 3, c))
    return [entry[1:] for entry in sorted(due)]


def kernel(
    top_bit, field, source_one, sections_one, target_one, source_two, sections_two, target_two, tables,
    out, x, sources, weights, targets, own, last, total,
    in_sems, out_sems, send_sems, recv_sems, node_send_sems, node_recv_sems, *landings,
):
    nodes, chunks = own.shape[3], own.shape[2]
    leaf = x.shape[1]
    g, h = lax.axis_index("grp"), lax.axis_index("half")

    landing = iter(landings)
    partner = {
        (level, s, c): next(landing)
        for level in (ONE, TWO) for s in range(SECTIONS) for c in range(chunks)
    }
    for level in (ONE, TWO):
        for c in range(chunks):
            partner[level, SECTIONS, c] = last.at[level, c]

    loads = {}

    def load(name, at, src, dst):
        loads[name] = pltpu.make_async_copy(src, dst, in_sems.at[at])
        loads[name].start()

    load("x", 0, field, x)
    load(("s", TWO), 1, source_two, sources.at[TWO])
    load(("s", ONE), 2, source_one, sources.at[ONE])
    for s in range(SECTIONS):
        load(("w", ONE, s), 3 + 2 * s, sections_one.at[s], weights.at[ONE, s])
        load(("w", TWO, s), 4 + 2 * s, sections_two.at[s], weights.at[TWO, s])
    load(("t", ONE), 9, target_one, targets.at[ONE])
    load(("t", TWO), 10, target_two, targets.at[TWO])

    def need(name):
        if name in loads:
            loads.pop(name).wait()

    peers = {}
    for s in range(SECTIONS):
        peers[ONE, s] = (flipped(g, top_bit - 1 - s), h)
        peers[TWO, s] = (flipped(g, top_bit - 2 - s), h)
    peers[ONE, SECTIONS] = (g, 1 - h)
    peers[TWO, SECTIONS] = (flipped(g, top_bit - 1), h)

    barrier = pltpu.get_barrier_semaphore()
    greeted = [peers[ONE, s] for s in range(STAGES)] + [peers[TWO, 2]]
    for peer in greeted:
        pl.semaphore_signal(barrier, inc=1, device_id=peer, device_id_type=MESH)

    def move(level, stage, c):
        return pltpu.make_async_remote_copy(
            src_ref=own.at[level, stage, c],
            dst_ref=partner[level, stage, c],
            send_sem=send_sems.at[level, stage, c],
            recv_sem=recv_sems.at[level, stage, c],
            device_id=peers[level, stage],
            device_id_type=MESH,
        )

    def move_node(c, n):
        return pltpu.make_async_remote_copy(
            src_ref=own.at[ONE, SECTIONS, c, n],
            dst_ref=last.at[ONE, c, n],
            send_sem=node_send_sems.at[c, n],
            recv_sem=node_recv_sems.at[c, n],
            device_id=peers[ONE, SECTIONS],
            device_id_type=MESH,
        )

    def start_leaves(level, c):
        need("x")
        need(("s", level))

        @pl.loop(0, nodes)
        def _(n):
            block = x[n, :, c * WIDTH : (c + 1) * WIDTH]
            own[level, 0, c, n] = jnp.dot(
                sources[level, n], block, preferred_element_type=jnp.float32
            ).astype(jnp.bfloat16)

    def section(level, s, c):
        need(("w", level, s))

        @pl.loop(0, nodes)
        def _(n):
            near = jnp.dot(
                weights[level, s, n, :, :leaf], own[level, s, c, n], preferred_element_type=jnp.float32
            )
            far = jnp.dot(
                weights[level, s, n, :, leaf:],
                partner[level, s, c][tables[level, s, 0, 0, n]],
                preferred_element_type=jnp.float32,
            )
            own[level, s + 1, c, n] = (near + far).astype(jnp.bfloat16)
            if (level, s) == (ONE, SECTIONS - 1):
                move_node(c, n).start()

    def finish(c):
        need(("t", ONE))
        need(("t", TWO))
        move(TWO, SECTIONS, c).wait_recv()

        @pl.loop(0, nodes)
        def _(n):
            move_node(c, n).wait_recv()
            one = jnp.dot(
                targets[ONE, n], last[ONE, c, n], preferred_element_type=jnp.float32
            )
            two = jnp.dot(
                targets[TWO, n], last[TWO, c, n], preferred_element_type=jnp.float32
            )
            total[n, :, c * WIDTH : (c + 1) * WIDTH] = (one + two).astype(jnp.bfloat16)

        store(c).start()

    def store(c):
        columns = pl.ds(c * WIDTH, WIDTH)
        return pltpu.make_async_copy(total.at[:, :, columns], out.at[:, :, columns], out_sems.at[c])

    order = [(level, stage, c) for level, stage in CRITICAL for c in range(chunks)]
    ready, sent, received = set(), 0, 0
    greeting = [True]

    def greet():
        if greeting:
            greeting.pop()
            pl.semaphore_wait(barrier, len(greeted))

    def push():
        nonlocal sent
        while sent < len(order) and order[sent] in ready and sent < received + WINDOW:
            greet()
            move(*order[sent]).start()
            sent += 1

    for c in range(chunks):
        start_leaves(TWO, c)
        ready.add((TWO, 0, c))
        push()
        start_leaves(ONE, c)
        move(ONE, 0, c).start()
    for level, stage, c in arrivals(chunks):
        if (level, stage) == (ONE, SECTIONS):
            finish(c)
            continue
        move(level, stage, c).wait_recv()
        if (level, stage, c) in order:
            received += 1
            push()
        section(level, stage, c)
        ready.add((level, stage + 1, c))
        push()
        if (level, stage + 1) not in CRITICAL and (level, stage + 1) != (ONE, SECTIONS):
            move(level, stage + 1, c).start()

    for c in range(chunks):
        for level in (ONE, TWO):
            for stage in range(STAGES):
                if (level, stage) != (ONE, SECTIONS):
                    move(level, stage, c).wait_send()
        for n in range(nodes):
            move_node(c, n).wait_send()
        store(c).wait()


def on_device(
    field, source_one, sections_one, target_one, source_two, sections_two, target_two, pairing
):
    nodes, leaf = source_one.shape[2:4]
    columns = field.shape[3]
    chunks = columns // WIDTH
    top_bit = lax.axis_size("grp").bit_length() - 1
    anywhere = pl.BlockSpec(memory_space=pl.ANY)
    half = jnp.bfloat16
    blocks = (2, STAGES, chunks, nodes, leaf, WIDTH)
    result = pl.pallas_call(
        functools.partial(kernel, top_bit),
        out_shape=jax.ShapeDtypeStruct((nodes, leaf, columns), half),
        in_specs=[anywhere] * 7 + [pl.BlockSpec(memory_space=pltpu.SMEM)],
        out_specs=anywhere,
        scratch_shapes=[
            pltpu.VMEM((nodes, leaf, columns), half),
            pltpu.VMEM((2, nodes, leaf, leaf), half),
            pltpu.VMEM((2, SECTIONS, nodes, leaf, 2 * leaf), half),
            pltpu.VMEM((2, nodes, leaf, leaf), half),
            pltpu.VMEM(blocks, half),
            pltpu.VMEM((2, chunks, nodes, leaf, WIDTH), half),
            pltpu.VMEM((nodes, leaf, columns), half),
            pltpu.SemaphoreType.DMA((11,)),
            pltpu.SemaphoreType.DMA((chunks,)),
            pltpu.SemaphoreType.DMA((2, STAGES, chunks)),
            pltpu.SemaphoreType.DMA((2, STAGES, chunks)),
            pltpu.SemaphoreType.DMA((chunks, nodes)),
            pltpu.SemaphoreType.DMA((chunks, nodes)),
        ]
        + [pltpu.VMEM((nodes, leaf, WIDTH), half)] * (2 * SECTIONS * chunks),
        compiler_params=pltpu.CompilerParams(
            collective_id=0, has_side_effects=True, vmem_limit_bytes=56 << 20
        ),
        name="butterfly",
    )(
        field.reshape(nodes, leaf, columns),
        source_one[0, 0], sections_one[0, 0], target_one[0, 0],
        source_two[0, 0], sections_two[0, 0], target_two[0, 0],
        pairing,
    )
    return result.reshape(field.shape)


def solution(mesh):
    placed = (
        P("grp", "half", None, None),
        P("grp", "half", None, None, None),
        P("grp", "half", None, None, None, None),
        P("grp", "half", None, None, None),
        P("grp", "half", None, None, None),
        P("grp", "half", None, None, None, None),
        P("grp", "half", None, None, None),
        P(None, None, "grp", "half", None),
    )
    return jax.shard_map(
        on_device,
        mesh=mesh,
        in_specs=placed,
        out_specs=P("grp", "half", None, None),
        check_vma=False,
    )
```

time: 255 us -> 205 us (0.80); the launches traced: 253 us -> 205 us
  Pallas kernels: 0 us -> 203 us
  waiting for transfers between devices: 180 us -> 0 us
  starting transfers between devices: 37.7 us -> 0 us
  matrix products: 22.9 us -> 0 us
  local copies, waits for them, and re-layouts: 10.9 us -> 2.26 us
    pallas_call x0 -> x1, Pallas kernels: none -> 203 us  [on_device(): pl.pallas_call(functools.partial(kernel, top_bit), out_shape=jax.ShapeDty...]
    ppermute x8 -> x0, waiting for transfers between devices: 180 us -> none  [swapped(): lax.ppermute(value, axis, [(i, i ^ 1 << bit) for i in range(lax.axis_size...]
    ppermute x8 -> x0, starting transfers between devices: 37.7 us -> none  [swapped(): lax.ppermute(value, axis, [(i, i ^ 1 << bit) for i in range(lax.axis_size...]
    dot_general x10 -> x0, matrix products: 22.9 us -> none  [product(): jnp.einsum('nij,njc->nic', basis, blocks, preferred_element_type=jnp.floa...]
    gather x6 -> x0, local copies, waits for them, and re-layouts: 8.57 us -> none  [advance(): partner = jnp.take(partner, tables, axis=0)]
  transfers between devices with their start and end apart: 8 -> 0, of which waited for: 6 -> 0; matrix products, arithmetic and copies ran while one was open for 12% -> 0% of each run, Pallas kernels for 0% -> 0%
where the time goes in v1:
time: 205 us
  Pallas kernels  203 us (99%)
  local copies, waits for them, and re-layouts  2.26 us (1%)
    pallas_call x1, Pallas kernels, on_device(): pl.pallas_call(functools.partial(kernel, top_bit), out_shape=jax.ShapeDty...  203 us

profile of v1, /device:TPU:1, one launch (start us, length us, event | category | flops | bytes accessed | tf_op | source)
XLA Modules:
  0.0 205.3 jit_solution(7586412940939233380)
XLA Ops:
  0.0 203.0 %butterfly.1 = bf16[4,256,512]{2,1,0:T(8,128)(2,1)} custom-call(bf16[4,256,512]{2,1,0:T(8,128)(2,1)} %bitcast.11, bf16[4,256,256]{2,1,0:T(8,128)(2,1)} %bitcast.12, bf16[3,4,256,512]{3,2,1,0:T(8,128)(2,1)} %bitcast.9, bf16[4,256,256]{2,1,0:T(8,128)(2,1)} %bitcast.13, bf16[4,256,256]{2,1,0:T(8,128)(2,1)} %bitcast.14, bf16[3,4,256,512]{3,2,1,0:T(8,128)(2,1)} %bitcast.10, ...), custom_call_target="tpu_custom_call" | custom-call | tf_op jit(solution)/shard_map/butterfly/pallas_call | solution.py:214
  203.0 2.3 %copy.10 = bf16[1,1,1024,512]{3,2,1,0:T(8,128)(2,1)} copy(bf16[1,1,1024,512]{3,2,1,0:T(8,128)(2,1)} %bitcast.8) | data formatting | bytes 2097152

commit v2 on v1

--- a/solution.py
+++ b/solution.py
@@ -14,6 +14,7 @@
 WINDOW = 2
 ONE, TWO = 0, 1
 CRITICAL = ((TWO, 0), (ONE, 1), (TWO, 1), (ONE, 2))
+LENT = 3
 
 
 def flipped(index, bit):
@@ -31,15 +32,14 @@
         due.append((c + 1.0 + 0.1, ONE, 0, c))
         done = span * (2 * chunks + c + 1)
         due.append((done + 1.5 * span, TWO, 2, c))
-        done = span * (3 * chunks + c + 1)
-        due.append((done + 1.5 * span, ONE, 3, c))
+        due.append((span * (chunks + c + 1) + 1.5 * span, ONE, LENT, c))
     return [entry[1:] for entry in sorted(due)]
 
 
 def kernel(
     top_bit, field, source_one, sections_one, target_one, source_two, sections_two, target_two, tables,
-    out, x, sources, weights, targets, own, last, total,
-    in_sems, out_sems, send_sems, recv_sems, node_send_sems, node_recv_sems, *landings,
+    out, x, sources, weights, lent, targets, own, last, total, table, lent_table,
+    in_sems, out_sems, send_sems, recv_sems, lent_send_sems, lent_recv_sems, *landings,
 ):
     nodes, chunks = own.shape[3], own.shape[2]
     leaf = x.shape[1]
@@ -50,24 +50,33 @@
         (level, s, c): next(landing)
         for level in (ONE, TWO) for s in range(SECTIONS) for c in range(chunks)
     }
-    for level in (ONE, TWO):
-        for c in range(chunks):
-            partner[level, SECTIONS, c] = last.at[level, c]
+    for c in range(chunks):
+        partner[ONE, LENT, c] = last.at[ONE, c]
+        partner[TWO, SECTIONS, c] = last.at[TWO, c]
 
     loads = {}
 
-    def load(name, at, src, dst):
-        loads[name] = pltpu.make_async_copy(src, dst, in_sems.at[at])
+    def load(name, src, dst):
+        loads[name] = pltpu.make_async_copy(src, dst, in_sems.at[len(all_loads)])
+        all_loads.append(name)
         loads[name].start()
 
-    load("x", 0, field, x)
-    load(("s", TWO), 1, source_two, sources.at[TWO])
-    load(("s", ONE), 2, source_one, sources.at[ONE])
-    for s in range(SECTIONS):
-        load(("w", ONE, s), 3 + 2 * s, sections_one.at[s], weights.at[ONE, s])
-        load(("w", TWO, s), 4 + 2 * s, sections_two.at[s], weights.at[TWO, s])
-    load(("t", ONE), 9, target_one, targets.at[ONE])
-    load(("t", TWO), 10, target_two, targets.at[TWO])
+    all_loads = []
+    for c in range(chunks):
+        columns = pl.ds(c * WIDTH, WIDTH)
+        load(("x", c), field.at[:, :, columns], x.at[:, :, columns])
+        if c == 0:
+            load(("s", TWO), source_two, sources.at[TWO])
+            load(("s", ONE), source_one, sources.at[ONE])
+
+    def load_rest():
+        load("tables", tables, table)
+        for s in range(SECTIONS):
+            if s < SECTIONS - 1:
+                load(("w", ONE, s), sections_one.at[s], weights.at[ONE, s])
+            load(("w", TWO, s), sections_two.at[s], weights.at[TWO, s])
+        load(("t", ONE), target_one, targets.at[ONE])
+        load(("t", TWO), target_two, targets.at[TWO])
 
     def need(name):
         if name in loads:
@@ -77,17 +86,18 @@
     for s in range(SECTIONS):
         peers[ONE, s] = (flipped(g, top_bit - 1 - s), h)
         peers[TWO, s] = (flipped(g, top_bit - 2 - s), h)
-    peers[ONE, SECTIONS] = (g, 1 - h)
+    peers[ONE, LENT] = (g, 1 - h)
+    peers[ONE, SECTIONS - 1] = (peers[ONE, SECTIONS - 1][0], 1 - h)
     peers[TWO, SECTIONS] = (flipped(g, top_bit - 1), h)
 
     barrier = pltpu.get_barrier_semaphore()
-    greeted = [peers[ONE, s] for s in range(STAGES)] + [peers[TWO, 2]]
+    greeted = [peers[ONE, s] for s in range(STAGES)] + [peers[TWO, 1], peers[TWO, 2]]
     for peer in greeted:
         pl.semaphore_signal(barrier, inc=1, device_id=peer, device_id_type=MESH)
 
     def move(level, stage, c):
         return pltpu.make_async_remote_copy(
-            src_ref=own.at[level, stage, c],
+            src_ref=own.at[level, 2 if (level, stage) == (ONE, LENT) else stage, c],
             dst_ref=partner[level, stage, c],
             send_sem=send_sems.at[level, stage, c],
             recv_sem=recv_sems.at[level, stage, c],
@@ -95,18 +105,20 @@
             device_id_type=MESH,
         )
 
-    def move_node(c, n):
+    def lend(at, src, dst):
         return pltpu.make_async_remote_copy(
-            src_ref=own.at[ONE, SECTIONS, c, n],
-            dst_ref=last.at[ONE, c, n],
-            send_sem=node_send_sems.at[c, n],
-            recv_sem=node_recv_sems.at[c, n],
-            device_id=peers[ONE, SECTIONS],
+            src_ref=src,
+            dst_ref=dst,
+            send_sem=lent_send_sems.at[at],
+            recv_sem=lent_recv_sems.at[at],
+            device_id=peers[ONE, LENT],
             device_id_type=MESH,
         )
 
+    lending = [lend(0, sections_one.at[SECTIONS - 1], lent), lend(1, tables, lent_table)]
+
     def start_leaves(level, c):
-        need("x")
+        need(("x", c))
         need(("s", level))
 
         @pl.loop(0, nodes)
@@ -118,6 +130,7 @@
 
     def section(level, s, c):
         need(("w", level, s))
+        need("tables")
 
         @pl.loop(0, nodes)
         def _(n):
@@ -126,27 +139,27 @@
             )
             far = jnp.dot(
                 weights[level, s, n, :, leaf:],
-                partner[level, s, c][tables[level, s, 0, 0, n]],
+                partner[level, s, c][table[level, s, 0, 0, n]],
                 preferred_element_type=jnp.float32,
             )
             own[level, s + 1, c, n] = (near + far).astype(jnp.bfloat16)
-            if (level, s) == (ONE, SECTIONS - 1):
-                move_node(c, n).start()
 
     def finish(c):
         need(("t", ONE))
         need(("t", TWO))
-        move(TWO, SECTIONS, c).wait_recv()
 
         @pl.loop(0, nodes)
         def _(n):
-            move_node(c, n).wait_recv()
+            near = jnp.dot(lent[n, :, :leaf], last[ONE, c, n], preferred_element_type=jnp.float32)
+            far = jnp.dot(
+                lent[n, :, leaf:],
+                partner[ONE, 2, c][lent_table[ONE, 2, 0, 0, n]],
+                preferred_element_type=jnp.float32,
+            )
             one = jnp.dot(
-                targets[ONE, n], last[ONE, c, n], preferred_element_type=jnp.float32
-            )
-            two = jnp.dot(
-                targets[TWO, n], last[TWO, c, n], preferred_element_type=jnp.float32
-            )
+                targets[ONE, n], (near + far).astype(jnp.bfloat16), preferred_element_type=jnp.float32
+            )
+            two = jnp.dot(targets[TWO, n], last[TWO, c, n], preferred_element_type=jnp.float32)
             total[n, :, c * WIDTH : (c + 1) * WIDTH] = (one + two).astype(jnp.bfloat16)
 
         store(c).start()
@@ -177,27 +190,40 @@
         push()
         start_leaves(ONE, c)
         move(ONE, 0, c).start()
+        if c == 0:
+            load_rest()
     for level, stage, c in arrivals(chunks):
-        if (level, stage) == (ONE, SECTIONS):
-            finish(c)
-            continue
+        if (level, stage) == (ONE, 2):
+            move(TWO, SECTIONS, c).wait_recv()
+            if c == 0:
+                for copy in lending:
+                    copy.wait_recv()
         move(level, stage, c).wait_recv()
         if (level, stage, c) in order:
             received += 1
             push()
+        if (level, stage) == (ONE, LENT):
+            continue
+        if (level, stage) == (ONE, 2):
+            finish(c)
+            continue
         section(level, stage, c)
+        if (level, stage, c) == (ONE, 0, chunks - 1):
+            for copy in lending:
+                copy.start()
         ready.add((level, stage + 1, c))
         push()
-        if (level, stage + 1) not in CRITICAL and (level, stage + 1) != (ONE, SECTIONS):
+        if (level, stage) == (ONE, 1):
+            move(ONE, LENT, c).start()
+        if (level, stage + 1) not in CRITICAL:
             move(level, stage + 1, c).start()
 
+    for copy in lending:
+        copy.wait_send()
     for c in range(chunks):
         for level in (ONE, TWO):
             for stage in range(STAGES):
-                if (level, stage) != (ONE, SECTIONS):
-                    move(level, stage, c).wait_send()
-        for n in range(nodes):
-            move_node(c, n).wait_send()
+                move(level, stage, c).wait_send()
         store(c).wait()
 
 
@@ -214,22 +240,25 @@
     result = pl.pallas_call(
         functools.partial(kernel, top_bit),
         out_shape=jax.ShapeDtypeStruct((nodes, leaf, columns), half),
-        in_specs=[anywhere] * 7 + [pl.BlockSpec(memory_space=pltpu.SMEM)],
+        in_specs=[anywhere] * 8,
         out_specs=anywhere,
         scratch_shapes=[
             pltpu.VMEM((nodes, leaf, columns), half),
             pltpu.VMEM((2, nodes, leaf, leaf), half),
             pltpu.VMEM((2, SECTIONS, nodes, leaf, 2 * leaf), half),
+            pltpu.VMEM((nodes, leaf, 2 * leaf), half),
             pltpu.VMEM((2, nodes, leaf, leaf), half),
             pltpu.VMEM(blocks, half),
             pltpu.VMEM((2, chunks, nodes, leaf, WIDTH), half),
             pltpu.VMEM((nodes, leaf, columns), half),
-            pltpu.SemaphoreType.DMA((11,)),
+            pltpu.SMEM(pairing.shape, pairing.dtype),
+            pltpu.SMEM(pairing.shape, pairing.dtype),
+            pltpu.SemaphoreType.DMA((chunks + 2 + 1 + 2 * SECTIONS - 1 + 2,)),
             pltpu.SemaphoreType.DMA((chunks,)),
             pltpu.SemaphoreType.DMA((2, STAGES, chunks)),
             pltpu.SemaphoreType.DMA((2, STAGES, chunks)),
-            pltpu.SemaphoreType.DMA((chunks, nodes)),
-            pltpu.SemaphoreType.DMA((chunks, nodes)),
+            pltpu.SemaphoreType.DMA((2,)),
+            pltpu.SemaphoreType.DMA((2,)),
         ]
         + [pltpu.VMEM((nodes, leaf, WIDTH), half)] * (2 * SECTIONS * chunks),
         compiler_params=pltpu.CompilerParams(

time: 205 us -> 199 us (0.971)
  Pallas kernels: 203 us -> 197 us
    pallas_call x1, Pallas kernels: 203 us -> 197 us  [on_device(): pl.pallas_call(functools.partial(kernel, top_bit), out_shape=jax.ShapeDty...]
where the time goes in v2:
time: 199 us
  Pallas kernels  197 us (99%)
  local copies, waits for them, and re-layouts  2.26 us (1%)
    pallas_call x1, Pallas kernels, on_device(): pl.pallas_call(functools.partial(kernel, top_bit), out_shape=jax.ShapeDty...  197 us

profile of v2, /device:TPU:1, one launch (start us, length us, event | category | flops | bytes accessed | tf_op | source)
XLA Modules:
  0.0 198.8 jit_solution(12543993741604492761)
XLA Ops:
  0.0 196.6 %butterfly.1 = bf16[4,256,512]{2,1,0:T(8,128)(2,1)} custom-call(bf16[4,256,512]{2,1,0:T(8,128)(2,1)} %bitcast.11, bf16[4,256,256]{2,1,0:T(8,128)(2,1)} %bitcast.12, bf16[3,4,256,512]{3,2,1,0:T(8,128)(2,1)} %bitcast.9, bf16[4,256,256]{2,1,0:T(8,128)(2,1)} %bitcast.13, bf16[4,256,256]{2,1,0:T(8,128)(2,1)} %bitcast.14, bf16[3,4,256,512]{3,2,1,0:T(8,128)(2,1)} %bitcast.10, ...), custom_call_target="tpu_custom_call" | custom-call | tf_op jit(solution)/shard_map/butterfly/pallas_call | solution.py:240
  196.6 2.3 %copy.10 = bf16[1,1,1024,512]{3,2,1,0:T(8,128)(2,1)} copy(bf16[1,1,1024,512]{3,2,1,0:T(8,128)(2,1)} %bitcast.8) | data formatting | bytes 2097152

commit v3 on v2

--- a/solution.py
+++ b/solution.py
@@ -38,12 +38,25 @@
 
 def kernel(
     top_bit, field, source_one, sections_one, target_one, source_two, sections_two, target_two, tables,
-    out, x, sources, weights, lent, targets, own, last, total, table, lent_table,
+    out, x, sources, weights, lent, targets, own, last, near, one, two, total, table, lent_table,
     in_sems, out_sems, send_sems, recv_sems, lent_send_sems, lent_recv_sems, *landings,
 ):
     nodes, chunks = own.shape[3], own.shape[2]
     leaf = x.shape[1]
     g, h = lax.axis_index("grp"), lax.axis_index("half")
+
+    peers = {}
+    for s in range(SECTIONS):
+        peers[ONE, s] = (flipped(g, top_bit - 1 - s), h)
+        peers[TWO, s] = (flipped(g, top_bit - 2 - s), h)
+    peers[ONE, LENT] = (g, 1 - h)
+    peers[ONE, SECTIONS - 1] = (peers[ONE, SECTIONS - 1][0], 1 - h)
+    peers[TWO, SECTIONS] = (flipped(g, top_bit - 1), h)
+
+    barrier = pltpu.get_barrier_semaphore()
+    greeted = [peers[ONE, s] for s in range(STAGES)] + [peers[TWO, 1], peers[TWO, 2]]
+    for peer in greeted:
+        pl.semaphore_signal(barrier, inc=1, device_id=peer, device_id_type=MESH)
 
     landing = iter(landings)
     partner = {
@@ -81,19 +94,6 @@
     def need(name):
         if name in loads:
             loads.pop(name).wait()
-
-    peers = {}
-    for s in range(SECTIONS):
-        peers[ONE, s] = (flipped(g, top_bit - 1 - s), h)
-        peers[TWO, s] = (flipped(g, top_bit - 2 - s), h)
-    peers[ONE, LENT] = (g, 1 - h)
-    peers[ONE, SECTIONS - 1] = (peers[ONE, SECTIONS - 1][0], 1 - h)
-    peers[TWO, SECTIONS] = (flipped(g, top_bit - 1), h)
-
-    barrier = pltpu.get_barrier_semaphore()
-    greeted = [peers[ONE, s] for s in range(STAGES)] + [peers[TWO, 1], peers[TWO, 2]]
-    for peer in greeted:
-        pl.semaphore_signal(barrier, inc=1, device_id=peer, device_id_type=MESH)
 
     def move(level, stage, c):
         return pltpu.make_async_remote_copy(
@@ -144,31 +144,36 @@
             )
             own[level, s + 1, c, n] = (near + far).astype(jnp.bfloat16)
 
+    def prepare(c):
+        need(("t", TWO))
+
+        @pl.loop(0, nodes)
+        def _(n):
+            near[n] = jnp.dot(lent[n, :, :leaf], last[ONE, c, n], preferred_element_type=jnp.float32)
+            two[n] = jnp.dot(targets[TWO, n], last[TWO, c, n], preferred_element_type=jnp.float32)
+
     def finish(c):
         need(("t", ONE))
-        need(("t", TWO))
-
-        @pl.loop(0, nodes)
-        def _(n):
-            near = jnp.dot(lent[n, :, :leaf], last[ONE, c, n], preferred_element_type=jnp.float32)
+        for n in range(nodes):
             far = jnp.dot(
                 lent[n, :, leaf:],
                 partner[ONE, 2, c][lent_table[ONE, 2, 0, 0, n]],
                 preferred_element_type=jnp.float32,
             )
-            one = jnp.dot(
-                targets[ONE, n], (near + far).astype(jnp.bfloat16), preferred_element_type=jnp.float32
-            )
-            two = jnp.dot(targets[TWO, n], last[TWO, c, n], preferred_element_type=jnp.float32)
-            total[n, :, c * WIDTH : (c + 1) * WIDTH] = (one + two).astype(jnp.bfloat16)
-
-        store(c).start()
-
-    def store(c):
+            one[n] = (near[n] + far).astype(jnp.bfloat16)
+        for n in range(nodes):
+            product = jnp.dot(targets[ONE, n], one[n], preferred_element_type=jnp.float32)
+            total[n, :, c * WIDTH : (c + 1) * WIDTH] = (product + two[n]).astype(jnp.bfloat16)
+            store(c, n).start()
+
+    def store(c, n):
         columns = pl.ds(c * WIDTH, WIDTH)
-        return pltpu.make_async_copy(total.at[:, :, columns], out.at[:, :, columns], out_sems.at[c])
+        return pltpu.make_async_copy(total.at[n, :, columns], out.at[n, :, columns], out_sems.at[c, n])
 
     order = [(level, stage, c) for level, stage in CRITICAL for c in range(chunks)]
+    moves = [
+        (level, stage) for level in (ONE, TWO) for stage in range(STAGES) if (level, stage) != (ONE, 2)
+    ]
     ready, sent, received = set(), 0, 0
     greeting = [True]
 
@@ -198,6 +203,13 @@
             if c == 0:
                 for copy in lending:
                     copy.wait_recv()
+            prepare(c)
+            if c == chunks - 1:
+                for copy in lending:
+                    copy.wait_send()
+                for at in range(chunks):
+                    for there in moves:
+                        move(*there, at).wait_send()
         move(level, stage, c).wait_recv()
         if (level, stage, c) in order:
             received += 1
@@ -218,13 +230,10 @@
         if (level, stage + 1) not in CRITICAL:
             move(level, stage + 1, c).start()
 
-    for copy in lending:
-        copy.wait_send()
-    for c in range(chunks):
-        for level in (ONE, TWO):
-            for stage in range(STAGES):
-                move(level, stage, c).wait_send()
-        store(c).wait()
+    for c in range(chunks):
+        move(ONE, 2, c).wait_send()
+        for n in range(nodes):
+            store(c, n).wait()
 
 
 def on_device(
@@ -250,11 +259,14 @@
             pltpu.VMEM((2, nodes, leaf, leaf), half),
             pltpu.VMEM(blocks, half),
             pltpu.VMEM((2, chunks, nodes, leaf, WIDTH), half),
+            pltpu.VMEM((nodes, leaf, WIDTH), jnp.float32),
+            pltpu.VMEM((nodes, leaf, WIDTH), half),
+            pltpu.VMEM((nodes, leaf, WIDTH), jnp.float32),
             pltpu.VMEM((nodes, leaf, columns), half),
             pltpu.SMEM(pairing.shape, pairing.dtype),
             pltpu.SMEM(pairing.shape, pairing.dtype),
             pltpu.SemaphoreType.DMA((chunks + 2 + 1 + 2 * SECTIONS - 1 + 2,)),
-            pltpu.SemaphoreType.DMA((chunks,)),
+            pltpu.SemaphoreType.DMA((chunks, nodes)),
             pltpu.SemaphoreType.DMA((2, STAGES, chunks)),
             pltpu.SemaphoreType.DMA((2, STAGES, chunks)),
             pltpu.SemaphoreType.DMA((2,)),

time: 199 us -> 198 us (level)
  Pallas kernels: 197 us -> 195 us
where the time goes in v3:
time: 198 us
  Pallas kernels  195 us (98%)
  local copies, waits for them, and re-layouts  2.26 us (1%)
    pallas_call x1, Pallas kernels, on_device(): pl.pallas_call(functools.partial(kernel, top_bit), out_shape=jax.ShapeDty...  195 us

profile of v3, /device:TPU:1, one launch (start us, length us, event | category | flops | bytes accessed | tf_op | source)
XLA Modules:
  0.0 197.7 jit_solution(15758376277398960931)
XLA Ops:
  0.0 195.5 %butterfly.1 = bf16[4,256,512]{2,1,0:T(8,128)(2,1)} custom-call(bf16[4,256,512]{2,1,0:T(8,128)(2,1)} %bitcast.11, bf16[4,256,256]{2,1,0:T(8,128)(2,1)} %bitcast.12, bf16[3,4,256,512]{3,2,1,0:T(8,128)(2,1)} %bitcast.9, bf16[4,256,256]{2,1,0:T(8,128)(2,1)} %bitcast.13, bf16[4,256,256]{2,1,0:T(8,128)(2,1)} %bitcast.14, bf16[3,4,256,512]{3,2,1,0:T(8,128)(2,1)} %bitcast.10, ...), custom_call_target="tpu_custom_call" | custom-call | tf_op jit(solution)/shard_map/butterfly/pallas_call | solution.py:249
  195.5 2.3 %copy.10 = bf16[1,1,1024,512]{3,2,1,0:T(8,128)(2,1)} copy(bf16[1,1,1024,512]{3,2,1,0:T(8,128)(2,1)} %bitcast.8) | data formatting | bytes 2097152

commit v4 on v3

--- a/solution.py
+++ b/solution.py
@@ -38,10 +38,15 @@
 
 def kernel(
     top_bit, field, source_one, sections_one, target_one, source_two, sections_two, target_two, tables,
-    out, x, sources, weights, lent, targets, own, last, near, one, two, total, table, lent_table,
-    in_sems, out_sems, send_sems, recv_sems, lent_send_sems, lent_recv_sems, *landings,
+    *results_and_scratch,
 ):
-    nodes, chunks = own.shape[3], own.shape[2]
+    nodes = source_one.shape[0]
+    outs = results_and_scratch[:nodes]
+    (
+        x, sources, weights, lent, targets, own, last, near, one, two, table, lent_table,
+        in_sems, send_sems, recv_sems, lent_send_sems, lent_recv_sems, *landings,
+    ) = results_and_scratch[nodes:]
+    chunks = own.shape[2]
     leaf = x.shape[1]
     g, h = lax.axis_index("grp"), lax.axis_index("half")
 
@@ -163,12 +168,7 @@
             one[n] = (near[n] + far).astype(jnp.bfloat16)
         for n in range(nodes):
             product = jnp.dot(targets[ONE, n], one[n], preferred_element_type=jnp.float32)
-            total[n, :, c * WIDTH : (c + 1) * WIDTH] = (product + two[n]).astype(jnp.bfloat16)
-            store(c, n).start()
-
-    def store(c, n):
-        columns = pl.ds(c * WIDTH, WIDTH)
-        return pltpu.make_async_copy(total.at[n, :, columns], out.at[n, :, columns], out_sems.at[c, n])
+            outs[n][:, c * WIDTH : (c + 1) * WIDTH] = (product + two[n]).astype(jnp.bfloat16)
 
     order = [(level, stage, c) for level, stage in CRITICAL for c in range(chunks)]
     moves = [
@@ -232,8 +232,6 @@
 
     for c in range(chunks):
         move(ONE, 2, c).wait_send()
-        for n in range(nodes):
-            store(c, n).wait()
 
 
 def on_device(
@@ -246,11 +244,11 @@
     anywhere = pl.BlockSpec(memory_space=pl.ANY)
     half = jnp.bfloat16
     blocks = (2, STAGES, chunks, nodes, leaf, WIDTH)
-    result = pl.pallas_call(
+    results = pl.pallas_call(
         functools.partial(kernel, top_bit),
-        out_shape=jax.ShapeDtypeStruct((nodes, leaf, columns), half),
+        out_shape=[jax.ShapeDtypeStruct((leaf, columns), half)] * nodes,
         in_specs=[anywhere] * 8,
-        out_specs=anywhere,
+        out_specs=[pl.BlockSpec(memory_space=pltpu.VMEM)] * nodes,
         scratch_shapes=[
             pltpu.VMEM((nodes, leaf, columns), half),
             pltpu.VMEM((2, nodes, leaf, leaf), half),
@@ -262,11 +260,9 @@
             pltpu.VMEM((nodes, leaf, WIDTH), jnp.float32),
             pltpu.VMEM((nodes, leaf, WIDTH), half),
             pltpu.VMEM((nodes, leaf, WIDTH), jnp.float32),
-            pltpu.VMEM((nodes, leaf, columns), half),
             pltpu.SMEM(pairing.shape, pairing.dtype),
             pltpu.SMEM(pairing.shape, pairing.dtype),
             pltpu.SemaphoreType.DMA((chunks + 2 + 1 + 2 * SECTIONS - 1 + 2,)),
-            pltpu.SemaphoreType.DMA((chunks, nodes)),
             pltpu.SemaphoreType.DMA((2, STAGES, chunks)),
             pltpu.SemaphoreType.DMA((2, STAGES, chunks)),
             pltpu.SemaphoreType.DMA((2,)),
@@ -274,7 +270,7 @@
         ]
         + [pltpu.VMEM((nodes, leaf, WIDTH), half)] * (2 * SECTIONS * chunks),
         compiler_params=pltpu.CompilerParams(
-            collective_id=0, has_side_effects=True, vmem_limit_bytes=56 << 20
+            collective_id=0, has_side_effects=True, vmem_limit_bytes=105 << 19
         ),
         name="butterfly",
     )(
@@ -283,7 +279,7 @@
         source_two[0, 0], sections_two[0, 0], target_two[0, 0],
         pairing,
     )
-    return result.reshape(field.shape)
+    return jnp.concatenate(results, axis=0).reshape(field.shape)
 
 
 def solution(mesh):

time: 198 us -> 197 us (level)
  no operation moved by 1% of the time
where the time goes in v4:
time: 197 us; the launch traced here: 196 us
  Pallas kernels  195 us (99%)
    pallas_call x1, Pallas kernels, on_device(): pl.pallas_call(functools.partial(kernel, top_bit), out_shape=[jax.ShapeDt...  195 us

profile of v4, /device:TPU:1, one launch (start us, length us, event | category | flops | bytes accessed | tf_op | source)
XLA Modules:
  0.0 196.4 jit_solution(9634140153298709073)
XLA Ops:
  0.0 0.0 copy-start
  0.0 0.7 copy-done
  0.7 194.7 %butterfly.1 = (bf16[256,512]{1,0:T(8,128)(2,1)S(1)}, bf16[256,512]{1,0:T(8,128)(2,1)S(1)}, bf16[256,512]{1,0:T(8,128)(2,1)S(1)}, bf16[256,512]{1,0:T(8,128)(2,1)S(1)}) custom-call(bf16[4,256,512]{2,1,0:T(8,128)(2,1)} %bitcast.11, bf16[4,256,256]{2,1,0:T(8,128)(2,1)} %bitcast.12, bf16[3,4,256,512]{3,2,1,0:T(8,128)(2,1)} %bitcast.9, ...), custom_call_target="tpu_custom_call" | custom-call | tf_op jit(solution)/shard_map/butterfly/pallas_call | solution.py:247
  195.4 1.0 maximum_bitcast_fusion
Async XLA Ops:
  0.0 0.7 copy-start

commit v5 on v4

--- a/solution.py
+++ b/solution.py
@@ -55,11 +55,10 @@
         peers[ONE, s] = (flipped(g, top_bit - 1 - s), h)
         peers[TWO, s] = (flipped(g, top_bit - 2 - s), h)
     peers[ONE, LENT] = (g, 1 - h)
-    peers[ONE, SECTIONS - 1] = (peers[ONE, SECTIONS - 1][0], 1 - h)
     peers[TWO, SECTIONS] = (flipped(g, top_bit - 1), h)
 
     barrier = pltpu.get_barrier_semaphore()
-    greeted = [peers[ONE, s] for s in range(STAGES)] + [peers[TWO, 1], peers[TWO, 2]]
+    greeted = [peers[ONE, s] for s in range(STAGES)] + [peers[TWO, 2]]
     for peer in greeted:
         pl.semaphore_signal(barrier, inc=1, device_id=peer, device_id_type=MESH)
 
@@ -101,8 +100,13 @@
             loads.pop(name).wait()
 
     def move(level, stage, c):
+        source = own.at[level, stage, c]
+        if (level, stage) == (ONE, LENT):
+            source = own.at[ONE, 2, c]
+        if (level, stage) == (ONE, 2):
+            source = last.at[ONE, c]
         return pltpu.make_async_remote_copy(
-            src_ref=own.at[level, 2 if (level, stage) == (ONE, LENT) else stage, c],
+            src_ref=source,
             dst_ref=partner[level, stage, c],
             send_sem=send_sems.at[level, stage, c],
             recv_sem=recv_sems.at[level, stage, c],
@@ -215,6 +219,8 @@
             received += 1
             push()
         if (level, stage) == (ONE, LENT):
+            ready.add((ONE, 2, c))
+            push()
             continue
         if (level, stage) == (ONE, 2):
             finish(c)
@@ -223,10 +229,11 @@
         if (level, stage, c) == (ONE, 0, chunks - 1):
             for copy in lending:
                 copy.start()
+        if (level, stage) == (ONE, 1):
+            move(ONE, LENT, c).start()
+            continue
         ready.add((level, stage + 1, c))
         push()
-        if (level, stage) == (ONE, 1):
-            move(ONE, LENT, c).start()
         if (level, stage + 1) not in CRITICAL:
             move(level, stage + 1, c).start()
 

time: 197 us -> 194 us (0.985)
  Pallas kernels: 195 us -> 192 us
    pallas_call x1, Pallas kernels: 195 us -> 192 us  [on_device(): pl.pallas_call(functools.partial(kernel, top_bit), out_shape=[jax.ShapeDt...]
where the time goes in v5:
time: 194 us
  Pallas kernels  192 us (99%)
    pallas_call x1, Pallas kernels, on_device(): pl.pallas_call(functools.partial(kernel, top_bit), out_shape=[jax.ShapeDt...  192 us

profile of v5, /device:TPU:1, one launch (start us, length us, event | category | flops | bytes accessed | tf_op | source)
XLA Modules:
  0.0 194.1 jit_solution(11783831362120555171)
XLA Ops:
  0.0 0.0 copy-start
  0.0 0.7 copy-done
  0.7 192.3 %butterfly.1 = (bf16[256,512]{1,0:T(8,128)(2,1)S(1)}, bf16[256,512]{1,0:T(8,128)(2,1)S(1)}, bf16[256,512]{1,0:T(8,128)(2,1)S(1)}, bf16[256,512]{1,0:T(8,128)(2,1)S(1)}) custom-call(bf16[4,256,512]{2,1,0:T(8,128)(2,1)} %bitcast.11, bf16[4,256,256]{2,1,0:T(8,128)(2,1)} %bitcast.12, bf16[3,4,256,512]{3,2,1,0:T(8,128)(2,1)} %bitcast.9, ...), custom_call_target="tpu_custom_call" | custom-call | tf_op jit(solution)/shard_map/butterfly/pallas_call | solution.py:254
  193.0 1.0 maximum_bitcast_fusion
Async XLA Ops:
  0.0 0.7 copy-start

commit v6 on v5

--- a/solution.py
+++ b/solution.py
@@ -130,7 +130,7 @@
         need(("x", c))
         need(("s", level))
 
-        @pl.loop(0, nodes)
+        @pl.loop(0, nodes, unroll=c == 0)
         def _(n):
             block = x[n, :, c * WIDTH : (c + 1) * WIDTH]
             own[level, 0, c, n] = jnp.dot(

time: 194 us -> 194 us (level)
  no operation moved by 1% of the time
where the time goes in v6:
time: 194 us
  Pallas kernels  192 us (99%)
    pallas_call x1, Pallas kernels, on_device(): pl.pallas_call(functools.partial(kernel, top_bit), out_shape=[jax.ShapeDt...  192 us

profile of v6, /device:TPU:1, one launch (start us, length us, event | category | flops | bytes accessed | tf_op | source)
XLA Modules:
  0.0 194.1 jit_solution(13516058616703121966)
XLA Ops:
  0.0 0.0 copy-start
  0.0 0.7 copy-done
  0.7 192.3 %butterfly.1 = (bf16[256,512]{1,0:T(8,128)(2,1)S(1)}, bf16[256,512]{1,0:T(8,128)(2,1)S(1)}, bf16[256,512]{1,0:T(8,128)(2,1)S(1)}, bf16[256,512]{1,0:T(8,128)(2,1)S(1)}) custom-call(bf16[4,256,512]{2,1,0:T(8,128)(2,1)} %bitcast.11, bf16[4,256,256]{2,1,0:T(8,128)(2,1)} %bitcast.12, bf16[3,4,256,512]{3,2,1,0:T(8,128)(2,1)} %bitcast.9, ...), custom_call_target="tpu_custom_call" | custom-call | tf_op jit(solution)/shard_map/butterfly/pallas_call | solution.py:254
  193.0 1.0 maximum_bitcast_fusion
Async XLA Ops:
  0.0 0.7 copy-start

commit v7 on v5

--- a/solution.py
+++ b/solution.py
@@ -79,14 +79,17 @@
         loads[name].start()
 
     all_loads = []
-    for c in range(chunks):
+    def load_field(c):
         columns = pl.ds(c * WIDTH, WIDTH)
         load(("x", c), field.at[:, :, columns], x.at[:, :, columns])
-        if c == 0:
-            load(("s", TWO), source_two, sources.at[TWO])
-            load(("s", ONE), source_one, sources.at[ONE])
+
+    load_field(0)
+    load(("s", TWO), source_two, sources.at[TWO])
 
     def load_rest():
+        load(("s", ONE), source_one, sources.at[ONE])
+        for c in range(1, chunks):
+            load_field(c)
         load("tables", tables, table)
         for s in range(SECTIONS):
             if s < SECTIONS - 1:
@@ -197,10 +200,10 @@
         start_leaves(TWO, c)
         ready.add((TWO, 0, c))
         push()
+        if c == 0:
+            load_rest()
         start_leaves(ONE, c)
         move(ONE, 0, c).start()
-        if c == 0:
-            load_rest()
     for level, stage, c in arrivals(chunks):
         if (level, stage) == (ONE, 2):
             move(TWO, SECTIONS, c).wait_recv()

time: 194 us -> 194 us (level)
  no operation moved by 1% of the time
where the time goes in v7:
time: 194 us
  Pallas kernels  192 us (99%)
    pallas_call x1, Pallas kernels, on_device(): pl.pallas_call(functools.partial(kernel, top_bit), out_shape=[jax.ShapeDt...  192 us

profile of v7, /device:TPU:1, one launch (start us, length us, event | category | flops | bytes accessed | tf_op | source)
XLA Modules:
  0.0 194.1 jit_solution(2430258899015696412)
XLA Ops:
  0.0 0.0 copy-start
  0.0 0.7 copy-done
  0.7 192.3 %butterfly.1 = (bf16[256,512]{1,0:T(8,128)(2,1)S(1)}, bf16[256,512]{1,0:T(8,128)(2,1)S(1)}, bf16[256,512]{1,0:T(8,128)(2,1)S(1)}, bf16[256,512]{1,0:T(8,128)(2,1)S(1)}) custom-call(bf16[4,256,512]{2,1,0:T(8,128)(2,1)} %bitcast.11, bf16[4,256,256]{2,1,0:T(8,128)(2,1)} %bitcast.12, bf16[3,4,256,512]{3,2,1,0:T(8,128)(2,1)} %bitcast.9, ...), custom_call_target="tpu_custom_call" | custom-call | tf_op jit(solution)/shard_map/butterfly/pallas_call | solution.py:257
  193.0 1.0 maximum_bitcast_fusion
Async XLA Ops:
  0.0 0.7 copy-start
